TPU v7x, 256 devices: a whole 4x4x8 slice. The times are simulated.
256 devices in a mesh: rep: 4 (over x), fsdp: 64 (over z, y, core).
Axes of the slice: x: 4, y: 4, z: 8, core: 2. Of those that a mesh axis runs over, the one named last changes fastest.
Arguments:
- gradient: bfloat16 [192, 512, 512], P(None, 'fsdp'), may hold values from -10 to 10
- block_group: int32 [192], replicated, may hold values from 0 to 3, as said below
- block_owner: int32 [192], replicated, may hold values from 0 to 63, as said below
- left_kronecker: float32 [256, 512, 512], P(('rep', 'fsdp')), may hold values from -6 to 6
- right_kronecker: float32 [256, 512, 512], P(('rep', 'fsdp')), may hold values from -6 to 6
- left_root: bfloat16 [256, 512, 512], P(('rep', 'fsdp'))
- right_root: bfloat16 [256, 512, 512], P(('rep', 'fsdp'))
Outputs:
- new_left: float32 [256, 512, 512], P(('rep', 'fsdp'))
- new_right: float32 [256, 512, 512], P(('rep', 'fsdp'))
- update: bfloat16 [192, 512, 512], P(None, 'fsdp')
Inputs may be any that keep to these rules, and one draw needn't show every extreme that they name: `block_group`: together with block_owner, no pair of group and owner is named by more than 1 block, and some pair by exactly 1. `block_owner`: together with block_group, no pair of group and owner is named by more than 1 block, and some pair by exactly 1.
All inputs are finite; a program needn't handle non-finite values.
Results may differ from a plain program's by a relative error of at most 0.0049.
Values may be sent and summed in bfloat16 or wider, within the bound.
A program may use at most 64 MiB of HBM per device.

v0:
```python
import jax
import jax.numpy as jnp
from jax import lax
from jax.sharding import PartitionSpec as P

BLOCK_SIDE = 512


decay_rate = 0.9
epsilon = 1e-06


def per_device(
    gradient, block_group, block_owner, left_kronecker, right_kronecker, left_root, right_root
):
    fsdp_count = lax.axis_size("fsdp")
    replicas = lax.axis_size("rep")
    my_group = lax.axis_index("rep")
    block_count, strip_rows, block_width = gradient.shape
    count_of_slots = left_kronecker.shape[0]
    block_ids = jnp.arange(block_count, dtype=jnp.int32)
    earlier_twin = (
        (block_group[:, None] == block_group[None, :])
        & (block_owner[:, None] == block_owner[None, :])
        & (block_ids[None, :] < block_ids[:, None])
    )
    slot_rank = jnp.sum(earlier_twin.astype(jnp.int32), axis=1)
    slot_target = block_owner * count_of_slots + slot_rank
    inside_group = block_group == my_group
    wanted_slots = jnp.arange(fsdp_count * count_of_slots, dtype=jnp.int32)
    matches = inside_group[None, :] & (slot_target[None, :] == wanted_slots[:, None])
    present_slot = jnp.any(matches, axis=1)
    source_block = jnp.sum(jnp.where(matches, block_ids[None, :], 0), axis=1)
    outgoing = jnp.where(
        present_slot[:, None, None],
        jnp.take(gradient, source_block, axis=0),
        jnp.zeros((), gradient.dtype),
    )
    outgoing = outgoing.reshape(fsdp_count, count_of_slots, strip_rows, block_width)
    blocks = lax.all_to_all(outgoing, "fsdp", split_axis=0, concat_axis=2, tiled=True)[0]
    left_gram = jnp.einsum("sij,skj->sik", blocks, blocks, preferred_element_type=jnp.float32)
    right_gram = jnp.einsum("sji,sjk->sik", blocks, blocks, preferred_element_type=jnp.float32)
    new_left = decay_rate * left_kronecker + (1.0 - decay_rate) / BLOCK_SIDE * left_gram
    new_right = decay_rate * right_kronecker + (1.0 - decay_rate) / BLOCK_SIDE * right_gram
    partial_value = jnp.einsum(
        "sij,sjk->sik", left_root, blocks, preferred_element_type=jnp.float32
    ).astype(jnp.bfloat16)
    precond = jnp.einsum(
        "sij,sjk->sik", partial_value, right_root, preferred_element_type=jnp.float32
    )
    grad_wide = blocks.astype(jnp.float32)
    grad_norm = jnp.sqrt(jnp.sum(grad_wide * grad_wide, axis=(1, 2)))
    precond_norm = jnp.sqrt(jnp.sum(precond * precond, axis=(1, 2)) + epsilon)
    update_slots = (precond * (grad_norm / precond_norm)[:, None, None]).astype(jnp.bfloat16)
    everyone = lax.all_gather(update_slots[None], "rep", axis=0, tiled=True)
    pieces = lax.all_to_all(everyone[None], "fsdp", split_axis=3, concat_axis=0, tiled=True)
    flat_strips = pieces.reshape(fsdp_count * replicas * count_of_slots, strip_rows, block_width)
    pick_index = (block_owner * replicas + block_group) * count_of_slots + slot_rank
    result = jnp.take(flat_strips, pick_index, axis=0)
    return (new_left, new_right, result)


def solution(mesh):
    in_specs = (
        P(None, "fsdp", None),
        P(),
        P(),
        P(("rep", "fsdp"), None, None),
        P(("rep", "fsdp"), None, None),
        P(("rep", "fsdp"), None, None),
        P(("rep", "fsdp"), None, None),
    )
    out_specs = (
        P(("rep", "fsdp"), None, None),
        P(("rep", "fsdp"), None, None),
        P(None, "fsdp", None),
    )
    return jax.shard_map(
        per_device, mesh=mesh, in_specs=in_specs, out_specs=out_specs, check_vma=False
    )
```

profile of v0, /device:TPU:2, one launch (start us, length us, event | category | flops | bytes accessed | tf_op | source)
XLA Modules:
  0.0 156.6 jit_solution(12665085898743419668)
XLA Ops:
  7.2 0.0 copy-start
  7.2 0.0 all-gather.3.cloned.1.call-start
  7.2 1.0 convert_reduce_fusion
  8.3 0.7 add.48
  9.0 0.7 compare_and_fusion
  9.7 0.1 select_reduce_fusion
  9.8 0.1 fusion.18
  9.9 0.0 copy-done
  9.9 0.6 gather_fusion
  10.5 0.2 fusion.14
  10.8 29.6 %all_to_all.24 = bf16[64,1,8,512]{3,2,1,0:T(8,128)(2,1)S(1)} all-to-all(bf16[64,1,8,512]{3,2,1,0:T(8,128)(2,1)S(1)} %fusion.14), channel_id=1, replica_groups=mesh['rep'=4,'fsdp'=64] {'fsdp'}, dimensions={0} | all-to-all | bytes 1048576 | tf_op jit(solution)/shard_map/all_to_all | solution.py:40
  40.3 2.8 %multiply_reduce_fusion = (f32[]{:T(128)}, f32[512,512]{1,0:T(8,128)S(1)}) fusion(bf16[1,512,512]{2,1,0:T(8,128)(2,1)} %param.13, bf16[1,512,512]{2,1,0:T(8,128)(2,1)} %param.12, bf16[64,1,8,512]{3,2,1,0:T(8,128)(2,1)S(1)} %all_to_all.24), kind=kOutput, calls=%fused_computation.14 | convolution fusion | flops 537657344 | bytes 2621444 | tf_op jit(solution)/shard_map/sij,sjk->sik/dot_general | solution.py:48
  43.8 0.9 multiply_reduce_fusion.1
  45.4 0.9 multiply_convert_fusion
  46.3 0.0 all-gather.3.cloned.1.call-update
  46.3 29.2 %all-gather.3.cloned.1.call-done = bf16[2048,512]{1,0:T(8,128)(2,1)} async-done(((bf16[512,512]{1,0:T(8,128)(2,1)}), bf16[2048,512]{1,0:T(8,128)(2,1)}) %all-gather.3.cloned.1.call-update) | async-done | bytes 2097168 | tf_op jit(solution)/shard_map/all_gather | solution.py:55
  75.5 4.6 %copy.22 = bf16[1,4,1,512,512]{4,1,2,0,3:T(4,128)(2,1)} copy(bf16[1,4,1,512,512]{4,3,1,2,0:T(8,128)(2,1)} %bitcast.59) | data formatting | bytes 4194304 | tf_op jit(solution)/shard_map/broadcast_in_dim | solution.py:56
  80.1 0.0 copy-start.1
  80.1 10.9 %all-to-all-start.1 = ((bf16[1,4,1,512,512]{4,1,2,0,3:T(4,128)(2,1)}), bf16[1,4,1,512,512]{4,1,2,0,3:T(4,128)(2,1)}, u32[]{:S(2)}, u32[]{:S(2)}) async-start(bf16[1,4,1,512,512]{4,1,2,0,3:T(4,128)(2,1)} %copy.22), calls=%async_computation.1 | async-start | bytes 4194304 | tf_op jit(solution)/shard_map/all_to_all | solution.py:56
  91.0 0.0 copy-start.2
  91.0 0.0 copy-done.1
  91.0 1.4 fusion.3
  92.4 0.0 copy-done.2
  92.4 1.6 %fusion.4 = f32[1,512,512]{2,1,0:T(8,128)} fusion(f32[1,512,512]{2,1,0:T(8,128)S(1)} %copy-done.2, bf16[64,1,8,512]{3,2,1,0:T(8,128)(2,1)S(1)} %all_to_all.24), kind=kOutput, calls=%fused_computation.10 | convolution fusion | flops 269221888 | bytes 2621440 | tf_op jit(solution)/shard_map/sji,sjk->sik/dot_general | solution.py:42
  94.1 48.1 %all-to-all-done.1 = bf16[1,4,1,512,512]{4,1,2,0,3:T(4,128)(2,1)} async-done(((bf16[1,4,1,512,512]{4,1,2,0,3:T(4,128)(2,1)}), bf16[1,4,1,512,512]{4,1,2,0,3:T(4,128)(2,1)}, u32[]{:S(2)}, u32[]{:S(2)}) %all-to-all-start.1) | async-done | bytes 2097184 | tf_op jit(solution)/shard_map/all_to_all | solution.py:56
  142.2 2.0 %copy.30 = bf16[1,4,1,512,512]{4,3,1,2,0:T(8,128)(2,1)S(1)} copy(bf16[1,4,1,512,512]{4,1,2,0,3:T(4,128)(2,1)} %all-to-all-done.1) | data formatting | bytes 4194304 | tf_op jit(solution)/shard_map/all_to_all | solution.py:56
  144.2 1.7 %copy.24 = bf16[64,1,4,1,8,512]{5,4,2,0,3,1:T(8,128)(2,1)} copy(bf16[64,1,4,1,8,512]{5,4,0,2,3,1:T(8,128)(2,1)S(1)} %bitcast.57) | data formatting | bytes 4194304 | tf_op jit(solution)/shard_map/all_to_all | solution.py:56
  145.8 2.5 %gather_fusion.1 = bf16[192,8,512]{2,1,0:T(8,128)(2,1)S(1)} fusion(bf16[256,8,512]{2,1,0:T(8,128)(2,1)} %bitcast.58, s32[1024]{0:T(1024)S(1)} %pad_clamp_fusion), kind=kCustom, calls=%fused_computation.1 | custom fusion | bytes 3146496 | tf_op jit(solution)/shard_map/jit(_take)/gather | solution.py:59
  148.3 1.4 broadcast_select_fusion
  (4 shorter events, 0.0 us)
Async XLA Ops:
  7.2 2.8 %copy-start = (bf16[192,8,512]{2,1,0:T(8,128)(2,1)S(1)}, bf16[192,8,512]{2,1,0:T(8,128)(2,1)}, u32[]{:S(2)}) copy-start(bf16[192,8,512]{2,1,0:T(8,128)(2,1)} %param.7) | copy-start | bytes 4718596
  7.2 68.3 %all-gather.3.cloned.1.call-start = ((), (), s32[]{:S(2)}) async-start(), calls=%async_computation.2 | async-start | bytes 2621440 | tf_op jit(solution)/shard_map/all_gather | solution.py:55
  80.1 10.9 %copy-start.1 = (f32[1,512,512]{2,1,0:T(8,128)S(1)}, f32[1,512,512]{2,1,0:T(8,128)}, u32[]{:S(2)}) copy-start(f32[1,512,512]{2,1,0:T(8,128)} %param.10) | copy-start | bytes 3145732
  80.1 62.1 %all-to-all-start.1 = ((bf16[1,4,1,512,512]{4,1,2,0,3:T(4,128)(2,1)}), bf16[1,4,1,512,512]{4,1,2,0,3:T(4,128)(2,1)}, u32[]{:S(2)}, u32[]{:S(2)}) async-start(bf16[1,4,1,512,512]{4,1,2,0,3:T(4,128)(2,1)} %copy.22), calls=%async_computation.1 | async-start | bytes 4194304 | tf_op jit(solution)/shard_map/all_to_all | solution.py:56
  91.0 1.5 copy-start.2
Sparse Core Ops, SparseCore 0:
  46.4 29.0 all-gather.2
where the time goes:
time: 158 us; the launch traced here: 157 us
  waiting for transfers between devices  77.3 us (49%)
  blocking collectives  29.6 us (19%)
  between operations  15.5 us (10%)
  local copies, waits for them, and re-layouts  11.3 us (7%)
  starting transfers between devices  10.9 us (7%)
  other arithmetic  6.09 us (4%)
  matrix products  5.85 us (4%)
    all_to_all x1, waiting for transfers between devices, per_device(): lax.all_to_all(everyone[None], 'fsdp', split_axis=3, concat_axis=0, tiled...  48.1 us
    all_to_all x1, blocking collectives, per_device(): lax.all_to_all(outgoing, 'fsdp', split_axis=0, concat_axis=2, tiled=True)[0]  29.6 us
    all_gather x1, waiting for transfers between devices, per_device(): everyone = lax.all_gather(update_slots[None], 'rep', axis=0, tiled=True)  29.2 us
    all_to_all x1, starting transfers between devices, per_device(): lax.all_to_all(everyone[None], 'fsdp', split_axis=3, concat_axis=0, tiled...  10.9 us
    broadcast_in_dim x1, local copies, waits for them, and re-layouts, per_device(): everyone[None]  4.56 us
    all_to_all x2, local copies, waits for them, and re-layouts, per_device(): lax.all_to_all(everyone[None], 'fsdp', split_axis=3, concat_axis=0, tiled...  3.66 us
  transfers between devices with their start and end apart: 2, of which 2 were waited for; matrix products, arithmetic and copies ran while one was open for 2% of the time, Pallas kernels for 0%

commit v1 on v0

v1 whole, which is shorter than its diff:
```python
import jax
import jax.numpy as jnp
from jax import lax
from jax.experimental import pallas as pl
from jax.experimental.pallas import tpu as pltpu
from jax.sharding import PartitionSpec as P

BLOCK_SIDE = 512
NREP = 4
NZ = 8
NYC = 8
NF = NZ * NYC
ROWS = 8
NBLK = 192

decay_rate = 0.9
epsilon = 1e-06
MESH = pl.DeviceIdType.MESH
DMA = pltpu.SemaphoreType.DMA
bf16 = jnp.bfloat16
f32 = jnp.float32

FAR_FIRST = (4, 3, 5, 2, 6, 1, 7, 0)
NEAR_FIRST = (0, 1, 7, 2, 6, 3, 5, 4)


def step_kernel(
    src_ref, coef_ref, grad_hbm, lk_hbm, rk_hbm, lroot_hbm, rroot_hbm,
    all_ref, nl_ref, nr_ref,
    grad, outgoing, landed, lk, rk, lroot, rroot, upd,
    in_sem, send1, recv1, send2, recv2, sendx, recvx, sendr, recvr,
):
    rep = lax.axis_index("rep")
    me = lax.axis_index("fsdp")
    z = me // NYC
    yc = me % NYC
    right = (rep + 1) % NREP
    left = (rep + NREP - 1) % NREP

    barrier = pltpu.get_barrier_semaphore()

    @pl.loop(1, NF)
    def _(s):
        pl.semaphore_signal(
            barrier, inc=1, device_id={"fsdp": lax.rem(me + s, NF)}, device_id_type=MESH
        )

    for peer in (left, right):
        pl.semaphore_signal(barrier, inc=1, device_id={"rep": peer}, device_id_type=MESH)

    pairs = ((grad_hbm, grad), (lroot_hbm, lroot), (rroot_hbm, rroot), (lk_hbm, lk), (rk_hbm, rk))
    loads = [pltpu.make_async_copy(a, b, in_sem.at[i]) for i, (a, b) in enumerate(pairs)]
    for load in loads:
        load.start()
    loads[0].wait()

    @pl.loop(0, NF)
    def _(o):
        outgoing[o] = grad[src_ref[o]]

    pl.semaphore_wait(barrier, NF + 1)

    for d in FAR_FIRST:
        @pl.loop(0, NYC)
        def _(j):
            target = lax.rem(z + d, NZ) * NYC + lax.rem(yc + j, NYC)

            def go():
                pltpu.make_async_remote_copy(
                    src_ref=outgoing.at[target], dst_ref=landed.at[me],
                    send_sem=send1, recv_sem=recv1,
                    device_id={"fsdp": target}, device_id_type=MESH,
                ).start()

            if d == 0:
                pl.when(j > 0)(go)
            else:
                go()

    landed[me] = outgoing[me]
    loads[1].wait()
    loads[2].wait()
    whole1 = pltpu.make_async_remote_copy(
        src_ref=outgoing.at[pl.ds(0, NF - 1)], dst_ref=landed.at[pl.ds(0, NF - 1)],
        send_sem=send1, recv_sem=recv1, device_id={"fsdp": me}, device_id_type=MESH,
    )
    whole1.wait_recv()

    g = landed[...].reshape(BLOCK_SIDE, BLOCK_SIDE)
    partial = jnp.dot(lroot[0], g, preferred_element_type=f32).astype(bf16)
    precond = jnp.dot(partial, rroot[0], preferred_element_type=f32)
    wide = g.astype(f32)
    grad_norm = jnp.sqrt(jnp.sum(wide * wide, keepdims=True))
    precond_norm = jnp.sqrt(jnp.sum(precond * precond, keepdims=True) + epsilon)
    update = (precond * (grad_norm / precond_norm)).astype(bf16)
    upd[...] = update.reshape(NF, ROWS, BLOCK_SIDE)

    for i, d in enumerate(NEAR_FIRST):
        @pl.loop(0, NYC)
        def _(j):
            target = lax.rem(z + d, NZ) * NYC + lax.rem(yc + j, NYC)

            def go():
                pltpu.make_async_remote_copy(
                    src_ref=upd.at[target], dst_ref=all_ref.at[rep, me],
                    send_sem=send2, recv_sem=recv2.at[i],
                    device_id={"fsdp": target}, device_id_type=MESH,
                ).start()

            if d == 0:
                pl.when(j > 0)(go)
            else:
                go()

    all_ref[rep, me] = upd[me]

    def chunk(group, i):
        source = lax.rem(z + NZ - NEAR_FIRST[i], NZ)
        return all_ref.at[group, pl.ds(source * NYC, NYC)]

    def own(i, way):
        return pltpu.make_async_remote_copy(
            src_ref=chunk(rep, i), dst_ref=chunk(rep, i),
            send_sem=sendx, recv_sem=recvx.at[i, way],
            device_id={"rep": (right, left)[way]}, device_id_type=MESH,
        )

    def relay(i):
        way = i % 2
        group = (left, right)[way]
        return pltpu.make_async_remote_copy(
            src_ref=chunk(group, i), dst_ref=chunk(group, i),
            send_sem=sendr, recv_sem=recvr.at[i],
            device_id={"rep": (right, left)[way]}, device_id_type=MESH,
        )

    def landed_chunk(i):
        n = NYC - 1 if i == 0 else NYC
        return pltpu.make_async_remote_copy(
            src_ref=upd.at[pl.ds(0, n)], dst_ref=all_ref.at[rep, pl.ds(0, n)],
            send_sem=send2, recv_sem=recv2.at[i], device_id={"fsdp": me}, device_id_type=MESH,
        )

    loads[3].wait()
    loads[4].wait()
    coef = coef_ref[0]
    half = BLOCK_SIDE // 2

    def left_piece(k):
        rows = landed[pl.ds(k * NF // 2, NF // 2)].reshape(half, BLOCK_SIDE)
        gram = lax.dot_general(
            rows, landed[...].reshape(BLOCK_SIDE, BLOCK_SIDE), (((1,), (1,)), ((), ())),
            preferred_element_type=f32,
        )
        at = pl.ds(k * half, half)
        nl_ref[0, at, :] = decay_rate * lk[0, at, :] + coef * gram

    def right_piece(k):
        at = pl.ds(k * half, half)
        block = landed[...].reshape(BLOCK_SIDE, BLOCK_SIDE)
        gram = lax.dot_general(
            block[:, k * half:(k + 1) * half], block, (((0,), (0,)), ((), ())),
            preferred_element_type=f32,
        )
        nr_ref[0, at, :] = decay_rate * rk[0, at, :] + coef * gram

    work = {0: lambda: left_piece(0), 1: lambda: left_piece(1), 2: lambda: right_piece(0), 3: lambda: right_piece(1)}
    for i in range(NZ):
        landed_chunk(i).wait_recv()
        own(i, 0).start()
        own(i, 1).start()
        if i in work:
            work[i]()
        if i >= 1:
            own(i - 1, (i - 1) % 2).wait_recv()
            relay(i - 1).start()
    own(NZ - 1, (NZ - 1) % 2).wait_recv()
    relay(NZ - 1).start()
    for i in range(NZ):
        own(i, 1 - i % 2).wait_recv()
        relay(i).wait_recv()

    whole1.wait_send()
    pltpu.make_async_remote_copy(
        src_ref=upd.at[pl.ds(0, NF - 1)], dst_ref=all_ref.at[rep, pl.ds(0, NF - 1)],
        send_sem=send2, recv_sem=recv2.at[0], device_id={"fsdp": me}, device_id_type=MESH,
    ).wait_send()
    for i in range(NZ):
        own(i, 0).wait_send()
        own(i, 1).wait_send()
        relay(i).wait_send()


def finish_kernel(pick_ref, all_ref, nl_ref, nr_ref, out_hbm, nl_hbm, nr_hbm, out, sem):
    copies = [
        pltpu.make_async_copy(nl_ref, nl_hbm, sem.at[0]),
        pltpu.make_async_copy(nr_ref, nr_hbm, sem.at[1]),
    ]
    for c in copies:
        c.start()
    parts = 4
    n = NBLK // parts
    for p in range(parts):
        @pl.loop(p * n, (p + 1) * n, unroll=8)
        def _(b):
            out[b] = all_ref[pick_ref[b]]

        c = pltpu.make_async_copy(
            out.at[pl.ds(p * n, n)], out_hbm.at[pl.ds(p * n, n)], sem.at[2 + p]
        )
        c.start()
        copies.append(c)
    for c in copies:
        c.wait()


def per_device(
    gradient, block_group, block_owner, left_kronecker, right_kronecker, left_root, right_root
):
    my_group = lax.axis_index("rep")
    me = lax.axis_index("fsdp")
    block_ids = jnp.arange(NBLK, dtype=jnp.int32)
    key = block_group * NF + block_owner
    earlier_twin = (key[:, None] == key[None, :]) & (block_ids[None, :] < block_ids[:, None])
    position = key + jnp.sum(earlier_twin.astype(jnp.int32), axis=1)
    wanted = my_group * NF + jnp.arange(NF, dtype=jnp.int32)
    matches = position[None, :] == wanted[:, None]
    source = jnp.sum(jnp.where(matches, block_ids[None, :], 0), axis=1)
    present = jnp.any(position == my_group * NF + me)
    coef = jnp.where(present, (1.0 - decay_rate) / BLOCK_SIDE, 0.0).astype(f32).reshape(1)

    vmem = pl.BlockSpec(memory_space=pltpu.VMEM)
    smem = pl.BlockSpec(memory_space=pltpu.SMEM)
    anyspace = pl.BlockSpec(memory_space=pl.ANY)
    strips = (NF, ROWS, BLOCK_SIDE)
    square = (1, BLOCK_SIDE, BLOCK_SIDE)
    everything, nl, nr = pl.pallas_call(
        step_kernel,
        out_shape=(
            jax.ShapeDtypeStruct((NREP,) + strips, bf16),
            jax.ShapeDtypeStruct(square, f32),
            jax.ShapeDtypeStruct(square, f32),
        ),
        in_specs=[smem, smem] + [anyspace] * 5,
        out_specs=(vmem,) * 3,
        scratch_shapes=[
            pltpu.VMEM((NBLK, ROWS, BLOCK_SIDE), bf16),
            pltpu.VMEM(strips, bf16),
            pltpu.VMEM(strips, bf16),
            pltpu.VMEM(square, f32),
            pltpu.VMEM(square, f32),
            pltpu.VMEM(square, bf16),
            pltpu.VMEM(square, bf16),
            pltpu.VMEM(strips, bf16),
            DMA((5,)),
            DMA, DMA,
            DMA, DMA((NZ,)),
            DMA, DMA((NZ, 2)),
            DMA, DMA((NZ,)),
        ],
        name="shampoo_step",
        cost_estimate=pl.CostEstimate(
            flops=8 * BLOCK_SIDE**3, bytes_accessed=8 << 20, transcendentals=0
        ),
        compiler_params=pltpu.CompilerParams(
            collective_id=0, has_side_effects=True, vmem_limit_bytes=56 << 20
        ),
    )(source, coef, gradient, left_kronecker, right_kronecker, left_root, right_root)
    update, new_left, new_right = pl.pallas_call(
        finish_kernel,
        out_shape=(
            jax.ShapeDtypeStruct((NBLK, ROWS, BLOCK_SIDE), bf16),
            jax.ShapeDtypeStruct(square, f32),
            jax.ShapeDtypeStruct(square, f32),
        ),
        in_specs=[smem, vmem, vmem, vmem],
        out_specs=(anyspace,) * 3,
        scratch_shapes=[pltpu.VMEM((NBLK, ROWS, BLOCK_SIDE), bf16), DMA((6,))],
        name="place_update",
        compiler_params=pltpu.CompilerParams(vmem_limit_bytes=40 << 20),
    )(position, everything.reshape(NREP * NF, ROWS, BLOCK_SIDE), nl, nr)
    return (new_left, new_right, update)


def solution(mesh):
    in_specs = (
        P(None, "fsdp", None),
        P(),
        P(),
        P(("rep", "fsdp"), None, None),
        P(("rep", "fsdp"), None, None),
        P(("rep", "fsdp"), None, None),
        P(("rep", "fsdp"), None, None),
    )
    out_specs = (
        P(("rep", "fsdp"), None, None),
        P(("rep", "fsdp"), None, None),
        P(None, "fsdp", None),
    )
    return jax.shard_map(
        per_device, mesh=mesh, in_specs=in_specs, out_specs=out_specs, check_vma=False
    )
```

time: 158 us -> 67.5 us (0.43)
  waiting for transfers between devices: 77.3 us -> 0 us
  Pallas kernels: 0 us -> 59.7 us
  blocking collectives: 29.6 us -> 0 us
  between operations: 15.5 us -> 1.32 us
  starting transfers between devices: 10.9 us -> 0 us
  local copies, waits for them, and re-layouts: 11.3 us -> 4.03 us
  matrix products: 5.85 us -> 0 us
  other arithmetic: 6.09 us -> 2.23 us
    pallas_call x0 -> x2, Pallas kernels: none -> 59.7 us  [the longest x1 57.3 us: per_device(): pl.pallas_call(step_kernel, out_shape=(jax.ShapeDtypeStruct((NREP,) + str...]
    all_to_all x1 -> x0, waiting for transfers between devices: 48.1 us -> none  [per_device(): lax.all_to_all(everyone[None], 'fsdp', split_axis=3, concat_axis=0, tiled...]
    all_to_all x1 -> x0, blocking collectives: 29.6 us -> none  [per_device(): lax.all_to_all(outgoing, 'fsdp', split_axis=0, concat_axis=2, tiled=True)[0]]
    all_gather x1 -> x0, waiting for transfers between devices: 29.2 us -> none  [per_device(): everyone = lax.all_gather(update_slots[None], 'rep', axis=0, tiled=True)]
    all_to_all x1 -> x0, starting transfers between devices: 10.9 us -> none  [per_device(): lax.all_to_all(everyone[None], 'fsdp', split_axis=3, concat_axis=0, tiled...]
    dot_general x3 -> x0, matrix products: 5.85 us -> none  [the longest x1 2.81 us: per_device(): jnp.einsum('sij,sjk->sik', partial_value, right_root, preferred_element_t...]
    broadcast_in_dim x1 -> x0, local copies, waits for them, and re-layouts: 4.56 us -> none  [per_device(): everyone[None]]
    unnamed x6, local copies, waits for them, and re-layouts: 0.02 us -> 4.03 us
  transfers between devices with their start and end apart: 2 -> 0, of which waited for: 2 -> 0; matrix products, arithmetic and copies ran while one was open for 2% -> 0% of each run, Pallas kernels for 0% -> 0%
where the time goes in v1:
time: 67.5 us; the launch traced here: 67.3 us
  Pallas kernels  59.7 us (88%)
  local copies, waits for them, and re-layouts  4.03 us (6%)
  other arithmetic  2.23 us (3%)
  between operations  1.32 us (2%)
    pallas_call x1, Pallas kernels, per_device(): pl.pallas_call(step_kernel, out_shape=(jax.ShapeDtypeStruct((NREP,) + str...  57.3 us
    unnamed x6, local copies, waits for them, and re-layouts  4.03 us
    pallas_call x1, Pallas kernels, per_device(): pl.pallas_call(finish_kernel, out_shape=(jax.ShapeDtypeStruct((NBLK, ROWS...  2.42 us

profile of v1, /device:TPU:2, one launch (start us, length us, event | category | flops | bytes accessed | tf_op | source)
XLA Modules:
  0.0 67.3 jit_solution(11721965549053934748)
XLA Ops:
  0.6 0.7 %multiply_add_fusion = s32[192]{0:T(256)S(1)} fusion(s32[192]{0:T(256)} %param.9, s32[192]{0:T(256)} %param.8), kind=kLoop, calls=%fused_computation.5 | loop fusion | flops 384 | bytes 2304 | tf_op jit(solution)/shard_map/add | solution.py:223
  1.3 0.2 convert_reduce_fusion
  1.5 0.6 compare_reduce_fusion
  2.8 0.7 %select_reduce_fusion.src_ref = s32[64]{0:T(128)} fusion(s32[192]{0:T(256)S(1)} %get-tuple-element.16.pick_ref, s32[64]{0:T(128)S(1)} %iota_add_fusion), kind=kLoop, calls=%fused_computation.3 | loop fusion | flops 36800 | bytes 1280 | tf_op jit(solution)/shard_map/reduce_sum | solution.py:228
  3.5 57.3 %shampoo_step.1 = (bf16[4,64,8,512]{3,2,1,0:T(8,128)(2,1)}, f32[1,512,512]{2,1,0:T(8,128)}, f32[1,512,512]{2,1,0:T(8,128)}) custom-call(s32[64]{0:T(128)} %select_reduce_fusion.src_ref, f32[1]{0:T(128)} %bitcast.coef_ref, bf16[192,8,512]{2,1,0:T(8,128)(2,1)} %grad_hbm.1, f32[1,512,512]{2,1,0:T(8,128)} %lk_hbm.1, f32[1,512,512]{2,1,0:T(8,128)} %rk_hbm.1, ...), custom_call_target="tpu_custom_call" | custom-call | flops 1073741824 | bytes 8388608 | tf_op jit(solution)/shard_map/shampoo_step/pallas_call | solution.py:237
  60.8 0.0 copy-start
  60.8 1.6 %copy-done = bf16[4,64,8,512]{3,2,1,0:T(8,128)(2,1)S(1)} copy-done((bf16[4,64,8,512]{3,2,1,0:T(8,128)(2,1)S(1)}, bf16[4,64,8,512]{3,2,1,0:T(8,128)(2,1)}, u32[]{:S(2)}) %copy-start) | copy-done | bytes 2097176
  62.4 0.0 copy-start.1
  62.4 1.2 %copy-done.1 = f32[1,512,512]{2,1,0:T(8,128)S(1)} copy-done((f32[1,512,512]{2,1,0:T(8,128)S(1)}, f32[1,512,512]{2,1,0:T(8,128)}, u32[]{:S(2)}) %copy-start.1) | copy-done | bytes 1048600
  63.6 0.0 copy-start.2
  63.6 1.2 %copy-done.2 = f32[1,512,512]{2,1,0:T(8,128)S(1)} copy-done((f32[1,512,512]{2,1,0:T(8,128)S(1)}, f32[1,512,512]{2,1,0:T(8,128)}, u32[]{:S(2)}) %copy-start.2) | copy-done | bytes 1048600
  64.9 2.4 %place_update.1 = (bf16[192,8,512]{2,1,0:T(8,128)(2,1)}, f32[1,512,512]{2,1,0:T(8,128)}, f32[1,512,512]{2,1,0:T(8,128)}) custom-call(s32[192]{0:T(256)S(1)} %get-tuple-element.16.pick_ref, bf16[256,8,512]{2,1,0:T(8,128)(2,1)S(1)} %bitcast.2, f32[1,512,512]{2,1,0:T(8,128)S(1)} %copy-done.1, f32[1,512,512]{2,1,0:T(8,128)S(1)} %copy-done.2), custom_call_target="tpu_custom_call" | custom-call | tf_op jit(solution)/shard_map/place_update/pallas_call | solution.py:269
  (1 shorter events, 0.0 us)
Async XLA Ops:
  60.8 1.6 %copy-start = (bf16[4,64,8,512]{3,2,1,0:T(8,128)(2,1)S(1)}, bf16[4,64,8,512]{3,2,1,0:T(8,128)(2,1)}, u32[]{:S(2)}) copy-start(bf16[4,64,8,512]{3,2,1,0:T(8,128)(2,1)} %get-tuple-element.9) | copy-start | bytes 6291460
  62.4 1.2 %copy-start.1 = (f32[1,512,512]{2,1,0:T(8,128)S(1)}, f32[1,512,512]{2,1,0:T(8,128)}, u32[]{:S(2)}) copy-start(f32[1,512,512]{2,1,0:T(8,128)} %get-tuple-element.10.nl_ref) | copy-start | bytes 3145732
  63.6 1.2 %copy-start.2 = (f32[1,512,512]{2,1,0:T(8,128)S(1)}, f32[1,512,512]{2,1,0:T(8,128)}, u32[]{:S(2)}) copy-start(f32[1,512,512]{2,1,0:T(8,128)} %get-tuple-element.11.nr_ref) | copy-start | bytes 3145732

commit v2 on v1

--- a/solution.py
+++ b/solution.py
@@ -263,9 +263,9 @@
             flops=8 * BLOCK_SIDE**3, bytes_accessed=8 << 20, transcendentals=0
         ),
         compiler_params=pltpu.CompilerParams(
-            collective_id=0, has_side_effects=True, vmem_limit_bytes=56 << 20
+            collective_id=0, has_side_effects=True, vmem_limit_bytes=32 << 20
         ),
-    )(source, coef, gradient, left_kronecker, right_kronecker, left_root, right_root)
+    )(source, coef, *[pltpu.with_memory_space_constraint(x, pltpu.HBM) for x in (gradient, left_kronecker, right_kronecker, left_root, right_root)])
     update, new_left, new_right = pl.pallas_call(
         finish_kernel,
         out_shape=(

time: 67.5 us -> 60.9 us (0.902)
  local copies, waits for them, and re-layouts: 4.03 us -> 0 us
  Pallas kernels: 59.7 us -> 57.8 us
    unnamed x6 -> x0, local copies, waits for them, and re-layouts: 4.03 us -> none
    pallas_call x1, Pallas kernels: 57.3 us -> 55.4 us  [per_device(): pl.pallas_call(step_kernel, out_shape=(jax.ShapeDtypeStruct((NREP,) + str...]
where the time goes in v2:
time: 60.9 us; the launch traced here: 60.8 us
  Pallas kernels  57.8 us (95%)
  other arithmetic  1.71 us (3%)
  between operations  1.31 us (2%)
    pallas_call x1, Pallas kernels, per_device(): pl.pallas_call(step_kernel, out_shape=(jax.ShapeDtypeStruct((NREP,) + str...  55.4 us
    pallas_call x1, Pallas kernels, per_device(): pl.pallas_call(finish_kernel, out_shape=(jax.ShapeDtypeStruct((NBLK, ROWS...  2.43 us

profile of v2, /device:TPU:2, one launch (start us, length us, event | category | flops | bytes accessed | tf_op | source)
XLA Modules:
  0.0 60.8 jit_solution(1162960279606053875)
XLA Ops:
  0.6 0.7 %multiply_add_fusion = s32[192]{0:T(256)S(1)} fusion(s32[192]{0:T(256)} %param.9, s32[192]{0:T(256)} %param.8), kind=kLoop, calls=%fused_computation.5 | loop fusion | flops 384 | bytes 2304 | tf_op jit(solution)/shard_map/add | solution.py:223
  1.3 0.2 convert_reduce_fusion
  1.5 0.6 %compare_reduce_fusion = (pred[]{:T(512)}, s32[192]{0:T(256)S(1)}) fusion(s32[]{:T(128)S(6)} %add.23, s32[192]{0:T(256)S(1)} %multiply_add_fusion, s32[192]{0:T(256)S(1)} %convert_reduce_fusion), kind=kLoop, calls=%fused_computation.4 | loop fusion | flops 575 | bytes 2309 | tf_op jit(solution)/shard_map/reduce_or | solution.py:229
  2.8 0.2 select_reduce_fusion.src_ref
  3.0 55.4 %shampoo_step.1 = (bf16[4,64,8,512]{3,2,1,0:T(8,128)(2,1)S(1)}, f32[1,512,512]{2,1,0:T(8,128)S(1)}, f32[1,512,512]{2,1,0:T(8,128)S(1)}) custom-call(s32[64]{0:T(128)S(1)} %select_reduce_fusion.src_ref, f32[1]{0:T(128)} %bitcast.coef_ref, bf16[192,8,512]{2,1,0:T(8,128)(2,1)} %grad_hbm.1, f32[1,512,512]{2,1,0:T(8,128)} %lk_hbm.1, f32[1,512,512]{2,1,0:T(8,128)} %rk_hbm.1, ...), custom_call_target="tpu_custom_call" | custom-call | flops 1073741824 | bytes 8388608 | tf_op jit(solution)/shard_map/shampoo_step/pallas_call | solution.py:237
  58.4 2.4 %place_update.1 = (bf16[192,8,512]{2,1,0:T(8,128)(2,1)}, f32[1,512,512]{2,1,0:T(8,128)}, f32[1,512,512]{2,1,0:T(8,128)}) custom-call(s32[192]{0:T(256)S(1)} %get-tuple-element.16.pick_ref, bf16[256,8,512]{2,1,0:T(8,128)(2,1)S(1)} %bitcast.2, f32[1,512,512]{2,1,0:T(8,128)S(1)} %get-tuple-element.10.nl_ref, f32[1,512,512]{2,1,0:T(8,128)S(1)} %get-tuple-element.11.nr_ref), custom_call_target="tpu_custom_call" | custom-call | tf_op jit(solution)/shard_map/place_update/pallas_call | solution.py:269
  (1 shorter events, 0.0 us)

commit v3 on v2

--- a/solution.py
+++ b/solution.py
@@ -25,8 +25,9 @@
 
 
 def step_kernel(
-    src_ref, coef_ref, grad_hbm, lk_hbm, rk_hbm, lroot_hbm, rroot_hbm,
-    all_ref, nl_ref, nr_ref,
+    group_hbm, owner_hbm, grad_hbm, lk_hbm, rk_hbm, lroot_hbm, rroot_hbm,
+    all_ref, nl_ref, nr_ref, pos_ref,
+    group, owner, source_row, source,
     grad, outgoing, landed, lk, rk, lroot, rroot, upd,
     in_sem, send1, recv1, send2, recv2, sendx, recvx, sendr, recvr,
 ):
@@ -48,15 +49,40 @@
     for peer in (left, right):
         pl.semaphore_signal(barrier, inc=1, device_id={"rep": peer}, device_id_type=MESH)
 
-    pairs = ((grad_hbm, grad), (lroot_hbm, lroot), (rroot_hbm, rroot), (lk_hbm, lk), (rk_hbm, rk))
+    pairs = (
+        (group_hbm, group), (owner_hbm, owner), (grad_hbm, grad),
+        (lroot_hbm, lroot), (rroot_hbm, rroot), (lk_hbm, lk), (rk_hbm, rk),
+    )
     loads = [pltpu.make_async_copy(a, b, in_sem.at[i]) for i, (a, b) in enumerate(pairs)]
     for load in loads:
         load.start()
     loads[0].wait()
-
-    @pl.loop(0, NF)
+    loads[1].wait()
+
+    key = group[...] * NF + owner[...]
+    c = lax.broadcasted_iota(jnp.int32, (NBLK, NBLK), 0)
+    b = lax.broadcasted_iota(jnp.int32, (NBLK, NBLK), 1)
+    key_column = jnp.sum(jnp.where(b == c, key, 0), axis=1, keepdims=True)
+    rank = jnp.sum(jnp.where((key_column == key) & (c < b), 1, 0), axis=0, keepdims=True)
+    position = key + rank
+    pos_ref[...] = position
+    slot = lax.broadcasted_iota(jnp.int32, (NF, NBLK), 0)
+    block = lax.broadcasted_iota(jnp.int32, (NF, NBLK), 1)
+    match = position == slot + rep * NF
+    source_column = jnp.sum(jnp.where(match, block, 0), axis=1, keepdims=True)
+    down = lax.broadcasted_iota(jnp.int32, (NF, 128), 0)
+    across = lax.broadcasted_iota(jnp.int32, (NF, 128), 1)
+    source_row[...] = jnp.sum(jnp.where(down == across, source_column, 0), axis=0, keepdims=True)
+    to_scalars = pltpu.make_async_copy(source_row, source, in_sem.at[7])
+    to_scalars.start()
+    present = jnp.sum(jnp.where(position == rep * NF + me, 1, 0), axis=1, keepdims=True)
+    coef = jnp.where(present > 0, (1.0 - decay_rate) / BLOCK_SIDE, 0.0).astype(f32)
+    to_scalars.wait()
+    loads[2].wait()
+
+    @pl.loop(0, NF, unroll=8)
     def _(o):
-        outgoing[o] = grad[src_ref[o]]
+        outgoing[o] = grad[source[0, o]]
 
     pl.semaphore_wait(barrier, NF + 1)
 
@@ -78,8 +104,8 @@
                 go()
 
     landed[me] = outgoing[me]
-    loads[1].wait()
-    loads[2].wait()
+    loads[3].wait()
+    loads[4].wait()
     whole1 = pltpu.make_async_remote_copy(
         src_ref=outgoing.at[pl.ds(0, NF - 1)], dst_ref=landed.at[pl.ds(0, NF - 1)],
         send_sem=send1, recv_sem=recv1, device_id={"fsdp": me}, device_id_type=MESH,
@@ -141,9 +167,8 @@
             send_sem=send2, recv_sem=recv2.at[i], device_id={"fsdp": me}, device_id_type=MESH,
         )
 
-    loads[3].wait()
-    loads[4].wait()
-    coef = coef_ref[0]
+    loads[5].wait()
+    loads[6].wait()
     half = BLOCK_SIDE // 2
 
     def left_piece(k):
@@ -191,19 +216,22 @@
         relay(i).wait_send()
 
 
-def finish_kernel(pick_ref, all_ref, nl_ref, nr_ref, out_hbm, nl_hbm, nr_hbm, out, sem):
+def finish_kernel(pos_ref, all_ref, nl_ref, nr_ref, out_hbm, nl_hbm, nr_hbm, out, pick, sem):
+    to_scalars = pltpu.make_async_copy(pos_ref, pick, sem.at[6])
+    to_scalars.start()
     copies = [
         pltpu.make_async_copy(nl_ref, nl_hbm, sem.at[0]),
         pltpu.make_async_copy(nr_ref, nr_hbm, sem.at[1]),
     ]
     for c in copies:
         c.start()
+    to_scalars.wait()
     parts = 4
     n = NBLK // parts
     for p in range(parts):
         @pl.loop(p * n, (p + 1) * n, unroll=8)
         def _(b):
-            out[b] = all_ref[pick_ref[b]]
+            out[b] = all_ref[pick[0, b]]
 
         c = pltpu.make_async_copy(
             out.at[pl.ds(p * n, n)], out_hbm.at[pl.ds(p * n, n)], sem.at[2 + p]
@@ -217,33 +245,25 @@
 def per_device(
     gradient, block_group, block_owner, left_kronecker, right_kronecker, left_root, right_root
 ):
-    my_group = lax.axis_index("rep")
-    me = lax.axis_index("fsdp")
-    block_ids = jnp.arange(NBLK, dtype=jnp.int32)
-    key = block_group * NF + block_owner
-    earlier_twin = (key[:, None] == key[None, :]) & (block_ids[None, :] < block_ids[:, None])
-    position = key + jnp.sum(earlier_twin.astype(jnp.int32), axis=1)
-    wanted = my_group * NF + jnp.arange(NF, dtype=jnp.int32)
-    matches = position[None, :] == wanted[:, None]
-    source = jnp.sum(jnp.where(matches, block_ids[None, :], 0), axis=1)
-    present = jnp.any(position == my_group * NF + me)
-    coef = jnp.where(present, (1.0 - decay_rate) / BLOCK_SIDE, 0.0).astype(f32).reshape(1)
-
     vmem = pl.BlockSpec(memory_space=pltpu.VMEM)
-    smem = pl.BlockSpec(memory_space=pltpu.SMEM)
     anyspace = pl.BlockSpec(memory_space=pl.ANY)
     strips = (NF, ROWS, BLOCK_SIDE)
     square = (1, BLOCK_SIDE, BLOCK_SIDE)
-    everything, nl, nr = pl.pallas_call(
+    everything, nl, nr, position = pl.pallas_call(
         step_kernel,
         out_shape=(
             jax.ShapeDtypeStruct((NREP,) + strips, bf16),
             jax.ShapeDtypeStruct(square, f32),
             jax.ShapeDtypeStruct(square, f32),
+            jax.ShapeDtypeStruct((1, NBLK), jnp.int32),
         ),
-        in_specs=[smem, smem] + [anyspace] * 5,
-        out_specs=(vmem,) * 3,
+        in_specs=[anyspace] * 7,
+        out_specs=(vmem,) * 4,
         scratch_shapes=[
+            pltpu.VMEM((1, NBLK), jnp.int32),
+            pltpu.VMEM((1, NBLK), jnp.int32),
+            pltpu.VMEM((1, 128), jnp.int32),
+            pltpu.SMEM((1, 128), jnp.int32),
             pltpu.VMEM((NBLK, ROWS, BLOCK_SIDE), bf16),
             pltpu.VMEM(strips, bf16),
             pltpu.VMEM(strips, bf16),
@@ -252,7 +272,7 @@
             pltpu.VMEM(square, bf16),
             pltpu.VMEM(square, bf16),
             pltpu.VMEM(strips, bf16),
-            DMA((5,)),
+            DMA((8,)),
             DMA, DMA,
             DMA, DMA((NZ,)),
             DMA, DMA((NZ, 2)),
@@ -265,7 +285,13 @@
         compiler_params=pltpu.CompilerParams(
             collective_id=0, has_side_effects=True, vmem_limit_bytes=32 << 20
         ),
-    )(source, coef, *[pltpu.with_memory_space_constraint(x, pltpu.HBM) for x in (gradient, left_kronecker, right_kronecker, left_root, right_root)])
+    )(*[
+        pltpu.with_memory_space_constraint(x, pltpu.HBM)
+        for x in (
+            block_group.reshape(1, NBLK), block_owner.reshape(1, NBLK), gradient,
+            left_kronecker, right_kronecker, left_root, right_root,
+        )
+    ])
     update, new_left, new_right = pl.pallas_call(
         finish_kernel,
         out_shape=(
@@ -273,9 +299,13 @@
             jax.ShapeDtypeStruct(square, f32),
             jax.ShapeDtypeStruct(square, f32),
         ),
-        in_specs=[smem, vmem, vmem, vmem],
+        in_specs=[vmem] * 4,
         out_specs=(anyspace,) * 3,
-        scratch_shapes=[pltpu.VMEM((NBLK, ROWS, BLOCK_SIDE), bf16), DMA((6,))],
+        scratch_shapes=[
+            pltpu.VMEM((NBLK, ROWS, BLOCK_SIDE), bf16),
+            pltpu.SMEM((1, NBLK), jnp.int32),
+            DMA((7,)),
+        ],
         name="place_update",
         compiler_params=pltpu.CompilerParams(vmem_limit_bytes=40 << 20),
     )(position, everything.reshape(NREP * NF, ROWS, BLOCK_SIDE), nl, nr)

time: 60.9 us -> 58.1 us (0.954)
  other arithmetic: 1.71 us -> 0 us
  between operations: 1.31 us -> 0.64 us
    add x2 -> x0, other arithmetic: 0.71 us -> none  [the longest x1 0.7 us: per_device(): key = block_group * NF + block_owner]
    reduce_or x1 -> x0, other arithmetic: 0.64 us -> none  [per_device(): present = jnp.any(position == my_group * NF + me)]
where the time goes in v3:
time: 58.1 us; the launch traced here: 58 us
  Pallas kernels  57.4 us (99%)
  between operations  0.64 us (1%)
    pallas_call x1, Pallas kernels, per_device(): pl.pallas_call(step_kernel, out_shape=(jax.ShapeDtypeStruct((NREP,) + str...  55.5 us
    pallas_call x1, Pallas kernels, per_device(): pl.pallas_call(finish_kernel, out_shape=(jax.ShapeDtypeStruct((NBLK, ROWS...  1.89 us

profile of v3, /device:TPU:2, one launch (start us, length us, event | category | flops | bytes accessed | tf_op | source)
XLA Modules:
  0.0 58.0 jit_solution(8268539865497367971)
XLA Ops:
  0.6 55.5 %shampoo_step.1 = (bf16[4,64,8,512]{3,2,1,0:T(8,128)(2,1)S(1)}, f32[1,512,512]{2,1,0:T(8,128)S(1)}, f32[1,512,512]{2,1,0:T(8,128)S(1)}, s32[1,192]{1,0:T(1,128)S(1)}) custom-call(s32[1,192]{1,0:T(1,128)} %bitcast.4, s32[1,192]{1,0:T(1,128)} %bitcast.5, bf16[192,8,512]{2,1,0:T(8,128)(2,1)} %grad_hbm.1, f32[1,512,512]{2,1,0:T(8,128)} %lk_hbm.1, ...), custom_call_target="tpu_custom_call" | custom-call | flops 1073741824 | bytes 8388608 | tf_op jit(solution)/shard_map/shampoo_step/pallas_call | solution.py:252
  56.1 1.9 %place_update.1 = (bf16[192,8,512]{2,1,0:T(8,128)(2,1)}, f32[1,512,512]{2,1,0:T(8,128)}, f32[1,512,512]{2,1,0:T(8,128)}) custom-call(s32[1,192]{1,0:T(1,128)S(1)} %get-tuple-element.10.pos_ref, bf16[256,8,512]{2,1,0:T(8,128)(2,1)S(1)} %bitcast.3, f32[1,512,512]{2,1,0:T(8,128)S(1)} %get-tuple-element.12.nl_ref, f32[1,512,512]{2,1,0:T(8,128)S(1)} %get-tuple-element.13.nr_ref), custom_call_target="tpu_custom_call" | custom-call | tf_op jit(solution)/shard_map/place_update/pallas_call | solution.py:295

commit v4 on v3

--- a/solution.py
+++ b/solution.py
@@ -20,8 +20,12 @@
 bf16 = jnp.bfloat16
 f32 = jnp.float32
 
-FAR_FIRST = (4, 3, 5, 2, 6, 1, 7, 0)
-NEAR_FIRST = (0, 1, 7, 2, 6, 3, 5, 4)
+FIRST_ORDER = (4, 3, 5, 2, 6, 1, 7, 0)
+OVER_FIRST = (0, 1, 7)
+ROUND_FIRST = (2, 6, 3, 5, 4)
+SPREAD_OWN_FIRST = False
+OPPOSITE_AT = 3
+WORK_AT = (-1, -1, 0, 1)
 
 
 def step_kernel(
@@ -30,6 +34,7 @@
     group, owner, source_row, source,
     grad, outgoing, landed, lk, rk, lroot, rroot, upd,
     in_sem, send1, recv1, send2, recv2, sendx, recvx, sendr, recvr,
+    crossed, send_o, recv_o, send_or, recv_or, send_s, recv_s,
 ):
     rep = lax.axis_index("rep")
     me = lax.axis_index("fsdp")
@@ -86,9 +91,9 @@
 
     pl.semaphore_wait(barrier, NF + 1)
 
-    for d in FAR_FIRST:
-        @pl.loop(0, NYC)
-        def _(j):
+    @pl.loop(0, NYC)
+    def _(j):
+        for d in FIRST_ORDER:
             target = lax.rem(z + d, NZ) * NYC + lax.rem(yc + j, NYC)
 
             def go():
@@ -121,16 +126,40 @@
     update = (precond * (grad_norm / precond_norm)).astype(bf16)
     upd[...] = update.reshape(NF, ROWS, BLOCK_SIDE)
 
-    for i, d in enumerate(NEAR_FIRST):
+    def remote(src, dst, send, recv, device):
+        return pltpu.make_async_remote_copy(
+            src_ref=src, dst_ref=dst, send_sem=send, recv_sem=recv,
+            device_id=device, device_id_type=MESH,
+        )
+
+    ways = ({"rep": right}, {"rep": left})
+    came_from = (left, right)
+    opposite = (rep + 2) % NREP
+
+    def plane_of(d):
+        return lax.rem(z + d, NZ)
+
+    def over(k, way):
+        return remote(
+            upd.at[pl.ds(plane_of(OVER_FIRST[k]) * NYC, NYC)], crossed.at[rep, k],
+            send_o, recv_o.at[k, way], ways[way],
+        )
+
+    def over_relay(k, way):
+        part = crossed.at[came_from[way], k, pl.ds(way * (NYC // 2), NYC // 2)]
+        return remote(part, part, send_or, recv_or.at[k, way], ways[way])
+
+    def spread(k, group, strip):
+        d = OVER_FIRST[k]
+
         @pl.loop(0, NYC)
         def _(j):
-            target = lax.rem(z + d, NZ) * NYC + lax.rem(yc + j, NYC)
+            t = lax.rem(yc + j, NYC)
 
             def go():
-                pltpu.make_async_remote_copy(
-                    src_ref=upd.at[target], dst_ref=all_ref.at[rep, me],
-                    send_sem=send2, recv_sem=recv2.at[i],
-                    device_id={"fsdp": target}, device_id_type=MESH,
+                remote(
+                    strip(t), all_ref.at[group, me], send_s, recv_s,
+                    {"fsdp": plane_of(d) * NYC + t},
                 ).start()
 
             if d == 0:
@@ -138,37 +167,61 @@
             else:
                 go()
 
-    all_ref[rep, me] = upd[me]
+        if d == 0:
+            all_ref[group, me] = strip(yc)[...]
+
+    def spread_own():
+        for k in range(len(OVER_FIRST)):
+            spread(k, rep, lambda t: upd.at[plane_of(OVER_FIRST[k]) * NYC + t])
+
+    for k in range(len(OVER_FIRST)):
+        over(k, 0).start()
+        over(k, 1).start()
+
+    if SPREAD_OWN_FIRST:
+        spread_own()
+
+    for i, d in enumerate(ROUND_FIRST):
+        @pl.loop(0, NYC)
+        def _(j):
+            target = plane_of(d) * NYC + lax.rem(yc + j, NYC)
+
+            def go():
+                remote(
+                    upd.at[target], all_ref.at[rep, me], send2, recv2.at[i], {"fsdp": target}
+                ).start()
+
+            if d == 0:
+                pl.when(j > 0)(go)
+            else:
+                go()
+
+        if d == 0:
+            all_ref[rep, me] = upd[me]
+
+    if not SPREAD_OWN_FIRST:
+        spread_own()
 
     def chunk(group, i):
-        source = lax.rem(z + NZ - NEAR_FIRST[i], NZ)
-        return all_ref.at[group, pl.ds(source * NYC, NYC)]
+        return all_ref.at[group, pl.ds(plane_of(NZ - ROUND_FIRST[i]) * NYC, NYC)]
 
     def own(i, way):
-        return pltpu.make_async_remote_copy(
-            src_ref=chunk(rep, i), dst_ref=chunk(rep, i),
-            send_sem=sendx, recv_sem=recvx.at[i, way],
-            device_id={"rep": (right, left)[way]}, device_id_type=MESH,
-        )
+        return remote(chunk(rep, i), chunk(rep, i), sendx, recvx.at[i, way], ways[way])
 
     def relay(i):
         way = i % 2
-        group = (left, right)[way]
-        return pltpu.make_async_remote_copy(
-            src_ref=chunk(group, i), dst_ref=chunk(group, i),
-            send_sem=sendr, recv_sem=recvr.at[i],
-            device_id={"rep": (right, left)[way]}, device_id_type=MESH,
-        )
-
-    def landed_chunk(i):
-        n = NYC - 1 if i == 0 else NYC
-        return pltpu.make_async_remote_copy(
-            src_ref=upd.at[pl.ds(0, n)], dst_ref=all_ref.at[rep, pl.ds(0, n)],
-            send_sem=send2, recv_sem=recv2.at[i], device_id={"fsdp": me}, device_id_type=MESH,
-        )
-
-    loads[5].wait()
-    loads[6].wait()
+        part = chunk(came_from[way], i)
+        return remote(part, part, sendr, recvr.at[i], ways[way])
+
+    def strips_of(d):
+        return NYC - 1 if d == 0 else NYC
+
+    def arrived(i):
+        n = strips_of(ROUND_FIRST[i])
+        return remote(
+            upd.at[pl.ds(0, n)], all_ref.at[rep, pl.ds(0, n)], send2, recv2.at[i], {"fsdp": me}
+        )
+
     half = BLOCK_SIDE // 2
 
     def left_piece(k):
@@ -189,28 +242,58 @@
         )
         nr_ref[0, at, :] = decay_rate * rk[0, at, :] + coef * gram
 
-    work = {0: lambda: left_piece(0), 1: lambda: left_piece(1), 2: lambda: right_piece(0), 3: lambda: right_piece(1)}
-    for i in range(NZ):
-        landed_chunk(i).wait_recv()
+    pieces = [lambda: left_piece(0), lambda: left_piece(1), lambda: right_piece(0), lambda: right_piece(1)]
+
+    def work(point):
+        for p, at in enumerate(WORK_AT):
+            if at == point:
+                pieces[p]()
+
+    loads[5].wait()
+    loads[6].wait()
+    work(-1)
+    for k in range(len(OVER_FIRST)):
+        for way in range(2):
+            over(k, way).wait_recv()
+            over_relay(k, way).start()
+            group = came_from[way]
+            spread(k, group, lambda t: crossed.at[group, k, t])
+    count = len(ROUND_FIRST)
+    for i in range(count):
+        arrived(i).wait_recv()
         own(i, 0).start()
         own(i, 1).start()
-        if i in work:
-            work[i]()
+        work(i)
         if i >= 1:
             own(i - 1, (i - 1) % 2).wait_recv()
             relay(i - 1).start()
-    own(NZ - 1, (NZ - 1) % 2).wait_recv()
-    relay(NZ - 1).start()
-    for i in range(NZ):
+        if i == OPPOSITE_AT:
+            for k in range(len(OVER_FIRST)):
+                over_relay(k, 0).wait_recv()
+                over_relay(k, 1).wait_recv()
+                spread(k, opposite, lambda t: crossed.at[opposite, k, t])
+    own(count - 1, (count - 1) % 2).wait_recv()
+    relay(count - 1).start()
+    for i in range(count):
         own(i, 1 - i % 2).wait_recv()
         relay(i).wait_recv()
+    if OVER_FIRST:
+        n = sum(strips_of(d) for d in OVER_FIRST)
+        strips = all_ref.at[:, pl.ds(0, n)]
+        whole = remote(strips, strips, send_s, recv_s, {"fsdp": me})
+        whole.wait_recv()
+        whole.wait_send()
 
     whole1.wait_send()
-    pltpu.make_async_remote_copy(
-        src_ref=upd.at[pl.ds(0, NF - 1)], dst_ref=all_ref.at[rep, pl.ds(0, NF - 1)],
-        send_sem=send2, recv_sem=recv2.at[0], device_id={"fsdp": me}, device_id_type=MESH,
+    n = sum(strips_of(d) for d in ROUND_FIRST)
+    remote(
+        upd.at[pl.ds(0, n)], all_ref.at[rep, pl.ds(0, n)], send2, recv2.at[0], {"fsdp": me}
     ).wait_send()
-    for i in range(NZ):
+    for k in range(len(OVER_FIRST)):
+        for way in range(2):
+            over(k, way).wait_send()
+            over_relay(k, way).wait_send()
+    for i in range(count):
         own(i, 0).wait_send()
         own(i, 1).wait_send()
         relay(i).wait_send()
@@ -277,6 +360,10 @@
             DMA, DMA((NZ,)),
             DMA, DMA((NZ, 2)),
             DMA, DMA((NZ,)),
+            pltpu.VMEM((NREP, NZ, NYC, ROWS, BLOCK_SIDE), bf16),
+            DMA, DMA((NZ, 2)),
+            DMA, DMA((NZ, 2)),
+            DMA, DMA,
         ],
         name="shampoo_step",
         cost_estimate=pl.CostEstimate(

time: 58.1 us -> 53.1 us (0.914); the launches traced: 58 us -> 52.4 us
  Pallas kernels: 57.4 us -> 51.7 us
    pallas_call x1, Pallas kernels: 55.5 us -> 49.8 us  [per_device(): pl.pallas_call(step_kernel, out_shape=(jax.ShapeDtypeStruct((NREP,) + str...]
where the time goes in v4:
time: 53.1 us; the launch traced here: 52.4 us
  Pallas kernels  51.7 us (97%)
  between operations  0.64 us (1%)
    pallas_call x1, Pallas kernels, per_device(): pl.pallas_call(step_kernel, out_shape=(jax.ShapeDtypeStruct((NREP,) + str...  49.8 us
    pallas_call x1, Pallas kernels, per_device(): pl.pallas_call(finish_kernel, out_shape=(jax.ShapeDtypeStruct((NBLK, ROWS...  1.89 us

profile of v4, /device:TPU:2, one launch (start us, length us, event | category | flops | bytes accessed | tf_op | source)
XLA Modules:
  0.0 52.4 jit_solution(1237659614932620279)
XLA Ops:
  0.6 49.8 %shampoo_step.1 = (bf16[4,64,8,512]{3,2,1,0:T(8,128)(2,1)S(1)}, f32[1,512,512]{2,1,0:T(8,128)S(1)}, f32[1,512,512]{2,1,0:T(8,128)S(1)}, s32[1,192]{1,0:T(1,128)S(1)}) custom-call(s32[1,192]{1,0:T(1,128)} %bitcast.4, s32[1,192]{1,0:T(1,128)} %bitcast.5, bf16[192,8,512]{2,1,0:T(8,128)(2,1)} %grad_hbm.1, f32[1,512,512]{2,1,0:T(8,128)} %lk_hbm.1, ...), custom_call_target="tpu_custom_call" | custom-call | flops 1073741824 | bytes 8388608 | tf_op jit(solution)/shard_map/shampoo_step/pallas_call | solution.py:335
  50.5 1.9 %place_update.1 = (bf16[192,8,512]{2,1,0:T(8,128)(2,1)}, f32[1,512,512]{2,1,0:T(8,128)}, f32[1,512,512]{2,1,0:T(8,128)}) custom-call(s32[1,192]{1,0:T(1,128)S(1)} %get-tuple-element.10.pos_ref, bf16[256,8,512]{2,1,0:T(8,128)(2,1)S(1)} %bitcast.3, f32[1,512,512]{2,1,0:T(8,128)S(1)} %get-tuple-element.12.nl_ref, f32[1,512,512]{2,1,0:T(8,128)S(1)} %get-tuple-element.13.nr_ref), custom_call_target="tpu_custom_call" | custom-call | tf_op jit(solution)/shard_map/place_update/pallas_call | solution.py:382

commit v5 on v4

--- a/solution.py
+++ b/solution.py
@@ -8,7 +8,9 @@
 BLOCK_SIDE = 512
 NREP = 4
 NZ = 8
-NYC = 8
+NY = 4
+NCORE = 2
+NYC = NY * NCORE
 NF = NZ * NYC
 ROWS = 8
 NBLK = 192
@@ -21,11 +23,14 @@
 f32 = jnp.float32
 
 FIRST_ORDER = (4, 3, 5, 2, 6, 1, 7, 0)
-OVER_FIRST = (0, 1, 7)
-ROUND_FIRST = (2, 6, 3, 5, 4)
+OVER_FIRST = (1, 7, 0)
+ROUND_FIRST = ((2, 6), (3, 5), (4,))
+Y_ORDER = (0, 1, 3, 2)
+SEND_ORDER = tuple((d, e) for together in ROUND_FIRST for d in together for e in Y_ORDER)
+LAG = 8
 SPREAD_OWN_FIRST = False
-OPPOSITE_AT = 3
-WORK_AT = (-1, -1, 0, 1)
+OPPOSITE_AT = 10
+WORK_AT = (-1, -1, -1, -1)
 
 
 def step_kernel(
@@ -40,26 +45,29 @@
     me = lax.axis_index("fsdp")
     z = me // NYC
     yc = me % NYC
+    y = yc // NCORE
+    core = yc % NCORE
     right = (rep + 1) % NREP
     left = (rep + NREP - 1) % NREP
 
     barrier = pltpu.get_barrier_semaphore()
+
+
+    for peer in (left, right):
+        pl.semaphore_signal(barrier, inc=1, device_id={"rep": peer}, device_id_type=MESH)
 
     @pl.loop(1, NF)
     def _(s):
         pl.semaphore_signal(
             barrier, inc=1, device_id={"fsdp": lax.rem(me + s, NF)}, device_id_type=MESH
         )
-
-    for peer in (left, right):
-        pl.semaphore_signal(barrier, inc=1, device_id={"rep": peer}, device_id_type=MESH)
 
     pairs = (
         (group_hbm, group), (owner_hbm, owner), (grad_hbm, grad),
         (lroot_hbm, lroot), (rroot_hbm, rroot), (lk_hbm, lk), (rk_hbm, rk),
     )
     loads = [pltpu.make_async_copy(a, b, in_sem.at[i]) for i, (a, b) in enumerate(pairs)]
-    for load in loads:
+    for load in loads[:3]:
         load.start()
     loads[0].wait()
     loads[1].wait()
@@ -108,6 +116,8 @@
             else:
                 go()
 
+    for load in loads[3:]:
+        load.start()
     landed[me] = outgoing[me]
     loads[3].wait()
     loads[4].wait()
@@ -181,46 +191,39 @@
     if SPREAD_OWN_FIRST:
         spread_own()
 
-    for i, d in enumerate(ROUND_FIRST):
-        @pl.loop(0, NYC)
-        def _(j):
-            target = plane_of(d) * NYC + lax.rem(yc + j, NYC)
-
-            def go():
-                remote(
-                    upd.at[target], all_ref.at[rep, me], send2, recv2.at[i], {"fsdp": target}
-                ).start()
-
-            if d == 0:
-                pl.when(j > 0)(go)
-            else:
-                go()
-
-        if d == 0:
-            all_ref[rep, me] = upd[me]
+    pairs = [(d, e) for together in ROUND_FIRST for e in Y_ORDER for d in together]
+    for n, (d, e) in enumerate(SEND_ORDER):
+        for c in range(NCORE):
+            target = plane_of(d) * NYC + lax.rem(y + e, NY) * NCORE + (core + c) % NCORE
+            remote(
+                upd.at[target], all_ref.at[rep, me], send2, recv2.at[pairs.index((d, e))],
+                {"fsdp": target},
+            ).start()
 
     if not SPREAD_OWN_FIRST:
         spread_own()
 
-    def chunk(group, i):
-        return all_ref.at[group, pl.ds(plane_of(NZ - ROUND_FIRST[i]) * NYC, NYC)]
-
-    def own(i, way):
-        return remote(chunk(rep, i), chunk(rep, i), sendx, recvx.at[i, way], ways[way])
-
-    def relay(i):
-        way = i % 2
-        part = chunk(came_from[way], i)
-        return remote(part, part, sendr, recvr.at[i], ways[way])
+    def chunk(group, n):
+        d, e = pairs[n]
+        start = plane_of(NZ - d) * NYC + lax.rem(y + NY - e, NY) * NCORE
+        return all_ref.at[group, pl.ds(start, NCORE)]
+
+    def own(n, way):
+        return remote(chunk(rep, n), chunk(rep, n), sendx, recvx.at[n, way], ways[way])
+
+    def relay(n):
+        way = n % 2
+        part = chunk(came_from[way], n)
+        return remote(part, part, sendr, recvr.at[n], ways[way])
+
+    def arrived(n):
+        return remote(
+            upd.at[pl.ds(0, NCORE)], all_ref.at[rep, pl.ds(0, NCORE)], send2, recv2.at[n],
+            {"fsdp": me},
+        )
 
     def strips_of(d):
         return NYC - 1 if d == 0 else NYC
-
-    def arrived(i):
-        n = strips_of(ROUND_FIRST[i])
-        return remote(
-            upd.at[pl.ds(0, n)], all_ref.at[rep, pl.ds(0, n)], send2, recv2.at[i], {"fsdp": me}
-        )
 
     half = BLOCK_SIDE // 2
 
@@ -258,25 +261,29 @@
             over_relay(k, way).start()
             group = came_from[way]
             spread(k, group, lambda t: crossed.at[group, k, t])
-    count = len(ROUND_FIRST)
-    for i in range(count):
-        arrived(i).wait_recv()
-        own(i, 0).start()
-        own(i, 1).start()
-        work(i)
-        if i >= 1:
-            own(i - 1, (i - 1) % 2).wait_recv()
-            relay(i - 1).start()
-        if i == OPPOSITE_AT:
+    count = len(pairs)
+
+    def pass_back(n):
+        own(n, n % 2).wait_recv()
+        relay(n).start()
+
+    for n in range(count):
+        arrived(n).wait_recv()
+        own(n, 0).start()
+        own(n, 1).start()
+        work(n)
+        if n >= LAG:
+            pass_back(n - LAG)
+        if n == OPPOSITE_AT:
             for k in range(len(OVER_FIRST)):
                 over_relay(k, 0).wait_recv()
                 over_relay(k, 1).wait_recv()
                 spread(k, opposite, lambda t: crossed.at[opposite, k, t])
-    own(count - 1, (count - 1) % 2).wait_recv()
-    relay(count - 1).start()
-    for i in range(count):
-        own(i, 1 - i % 2).wait_recv()
-        relay(i).wait_recv()
+    for n in range(max(count - LAG, 0), count):
+        pass_back(n)
+    for n in range(count):
+        own(n, 1 - n % 2).wait_recv()
+        relay(n).wait_recv()
     if OVER_FIRST:
         n = sum(strips_of(d) for d in OVER_FIRST)
         strips = all_ref.at[:, pl.ds(0, n)]
@@ -285,7 +292,7 @@
         whole.wait_send()
 
     whole1.wait_send()
-    n = sum(strips_of(d) for d in ROUND_FIRST)
+    n = NCORE * count
     remote(
         upd.at[pl.ds(0, n)], all_ref.at[rep, pl.ds(0, n)], send2, recv2.at[0], {"fsdp": me}
     ).wait_send()
@@ -293,10 +300,10 @@
         for way in range(2):
             over(k, way).wait_send()
             over_relay(k, way).wait_send()
-    for i in range(count):
-        own(i, 0).wait_send()
-        own(i, 1).wait_send()
-        relay(i).wait_send()
+    for n in range(count):
+        own(n, 0).wait_send()
+        own(n, 1).wait_send()
+        relay(n).wait_send()
 
 
 def finish_kernel(pos_ref, all_ref, nl_ref, nr_ref, out_hbm, nl_hbm, nr_hbm, out, pick, sem):
@@ -357,9 +364,9 @@
             pltpu.VMEM(strips, bf16),
             DMA((8,)),
             DMA, DMA,
-            DMA, DMA((NZ,)),
-            DMA, DMA((NZ, 2)),
-            DMA, DMA((NZ,)),
+            DMA, DMA((NZ * NY,)),
+            DMA, DMA((NZ * NY, 2)),
+            DMA, DMA((NZ * NY,)),
             pltpu.VMEM((NREP, NZ, NYC, ROWS, BLOCK_SIDE), bf16),
             DMA, DMA((NZ, 2)),
             DMA, DMA((NZ, 2)),

time: 53.1 us -> 52.2 us (0.983)
  Pallas kernels: 51.7 us -> 50.9 us
    pallas_call x1, Pallas kernels: 49.8 us -> 49 us  [per_device(): pl.pallas_call(step_kernel, out_shape=(jax.ShapeDtypeStruct((NREP,) + str...]
where the time goes in v5:
time: 52.2 us; the launch traced here: 51.5 us
  Pallas kernels  50.9 us (98%)
  between operations  0.64 us (1%)
    pallas_call x1, Pallas kernels, per_device(): pl.pallas_call(step_kernel, out_shape=(jax.ShapeDtypeStruct((NREP,) + str...  49 us
    pallas_call x1, Pallas kernels, per_device(): pl.pallas_call(finish_kernel, out_shape=(jax.ShapeDtypeStruct((NBLK, ROWS...  1.89 us

profile of v5, /device:TPU:2, one launch (start us, length us, event | category | flops | bytes accessed | tf_op | source)
XLA Modules:
  0.0 51.5 jit_solution(14371619882515306463)
XLA Ops:
  0.6 49.0 %shampoo_step.1 = (bf16[4,64,8,512]{3,2,1,0:T(8,128)(2,1)S(1)}, f32[1,512,512]{2,1,0:T(8,128)S(1)}, f32[1,512,512]{2,1,0:T(8,128)S(1)}, s32[1,192]{1,0:T(1,128)S(1)}) custom-call(s32[1,192]{1,0:T(1,128)} %bitcast.4, s32[1,192]{1,0:T(1,128)} %bitcast.5, bf16[192,8,512]{2,1,0:T(8,128)(2,1)} %grad_hbm.1, f32[1,512,512]{2,1,0:T(8,128)} %lk_hbm.1, ...), custom_call_target="tpu_custom_call" | custom-call | flops 1073741824 | bytes 8388608 | tf_op jit(solution)/shard_map/shampoo_step/pallas_call | solution.py:342
  49.7 1.9 %place_update.1 = (bf16[192,8,512]{2,1,0:T(8,128)(2,1)}, f32[1,512,512]{2,1,0:T(8,128)}, f32[1,512,512]{2,1,0:T(8,128)}) custom-call(s32[1,192]{1,0:T(1,128)S(1)} %get-tuple-element.10.pos_ref, bf16[256,8,512]{2,1,0:T(8,128)(2,1)S(1)} %bitcast.3, f32[1,512,512]{2,1,0:T(8,128)S(1)} %get-tuple-element.12.nl_ref, f32[1,512,512]{2,1,0:T(8,128)S(1)} %get-tuple-element.13.nr_ref), custom_call_target="tpu_custom_call" | custom-call | tf_op jit(solution)/shard_map/place_update/pallas_call | solution.py:389

commit v6 on v5

--- a/solution.py
+++ b/solution.py
@@ -28,6 +28,7 @@
 Y_ORDER = (0, 1, 3, 2)
 SEND_ORDER = tuple((d, e) for together in ROUND_FIRST for d in together for e in Y_ORDER)
 LAG = 8
+TAKE_AT = (-1, 1, 3)
 SPREAD_OWN_FIRST = False
 OPPOSITE_AT = 10
 WORK_AT = (-1, -1, -1, -1)
@@ -255,12 +256,16 @@
     loads[5].wait()
     loads[6].wait()
     work(-1)
-    for k in range(len(OVER_FIRST)):
+    def take_over(k):
         for way in range(2):
             over(k, way).wait_recv()
             over_relay(k, way).start()
             group = came_from[way]
             spread(k, group, lambda t: crossed.at[group, k, t])
+
+    for k in range(len(OVER_FIRST)):
+        if TAKE_AT[k] < 0:
+            take_over(k)
     count = len(pairs)
 
     def pass_back(n):
@@ -272,6 +277,9 @@
         own(n, 0).start()
         own(n, 1).start()
         work(n)
+        for k in range(len(OVER_FIRST)):
+            if TAKE_AT[k] == n:
+                take_over(k)
         if n >= LAG:
             pass_back(n - LAG)
         if n == OPPOSITE_AT:

time: 52.2 us -> 52.1 us (level)
  no operation moved by 1% of the time
where the time goes in v6:
time: 52.1 us; the launch traced here: 51.6 us
  Pallas kernels  51 us (98%)
  between operations  0.64 us (1%)
    pallas_call x1, Pallas kernels, per_device(): pl.pallas_call(step_kernel, out_shape=(jax.ShapeDtypeStruct((NREP,) + str...  49.1 us
    pallas_call x1, Pallas kernels, per_device(): pl.pallas_call(finish_kernel, out_shape=(jax.ShapeDtypeStruct((NBLK, ROWS...  1.89 us

profile of v6, /device:TPU:2, one launch (start us, length us, event | category | flops | bytes accessed | tf_op | source)
XLA Modules:
  0.0 51.6 jit_solution(4928008559822576064)
XLA Ops:
  0.6 49.1 %shampoo_step.1 = (bf16[4,64,8,512]{3,2,1,0:T(8,128)(2,1)S(1)}, f32[1,512,512]{2,1,0:T(8,128)S(1)}, f32[1,512,512]{2,1,0:T(8,128)S(1)}, s32[1,192]{1,0:T(1,128)S(1)}) custom-call(s32[1,192]{1,0:T(1,128)} %bitcast.4, s32[1,192]{1,0:T(1,128)} %bitcast.5, bf16[192,8,512]{2,1,0:T(8,128)(2,1)} %grad_hbm.1, f32[1,512,512]{2,1,0:T(8,128)} %lk_hbm.1, ...), custom_call_target="tpu_custom_call" | custom-call | flops 1073741824 | bytes 8388608 | tf_op jit(solution)/shard_map/shampoo_step/pallas_call | solution.py:350
  49.7 1.9 %place_update.1 = (bf16[192,8,512]{2,1,0:T(8,128)(2,1)}, f32[1,512,512]{2,1,0:T(8,128)}, f32[1,512,512]{2,1,0:T(8,128)}) custom-call(s32[1,192]{1,0:T(1,128)S(1)} %get-tuple-element.10.pos_ref, bf16[256,8,512]{2,1,0:T(8,128)(2,1)S(1)} %bitcast.3, f32[1,512,512]{2,1,0:T(8,128)S(1)} %get-tuple-element.12.nl_ref, f32[1,512,512]{2,1,0:T(8,128)S(1)} %get-tuple-element.13.nr_ref), custom_call_target="tpu_custom_call" | custom-call | tf_op jit(solution)/shard_map/place_update/pallas_call | solution.py:397
